TPU v7x, 32 devices: a whole 2x2x4 slice. The times are simulated.
32 devices in a mesh: groups: 2 (over x), mem: 8 (over z, y), tp: 2 (over core).
Axes of the slice: x: 2, y: 2, z: 4, core: 2. Of those that a mesh axis runs over, the one named last changes fastest.
Arguments:
- questions: bfloat16 [16, 32, 2048], P(('groups', 'mem'), None, 'tp'), parts along dimension 0
- memory: bfloat16 [128, 128, 2048], P('mem', None, 'tp')
- retrieved: int32 [16, 12], P(('groups', 'mem')), parts along dimension 0, may hold values from 0 to 127, as said below
- q_len: int32 [16], P(('groups', 'mem')), parts along dimension 0, may hold values from 8 to 32
- p_len: int32 [128], P('mem'), may hold values from 32 to 128
- norm_gain: bfloat16 [2048], replicated, may hold values from 0.099609375 to 1.8984375
- w_query: bfloat16 [2048, 2048], P(None, 'tp')
- w_key: bfloat16 [2048, 2048], P(None, 'tp')
- w_value: bfloat16 [2048, 2048], P(None, 'tp'), may hold values from -0.125 to 0.125
- w_out: bfloat16 [2048, 2048], P('tp'), may hold values from -0.75 to 0.75
Outputs:
- encoded: bfloat16 [16, 12, 160, 2048], P(('groups', 'mem'), None, None, 'tp'), parts along dimension 0
There are 2 independent parts, one for each index of `groups`. A program takes and returns all parts, laid end to end along the dimension named above; an argument that names none is the same for every part. Nothing has to cross between parts.
Inputs may be any that keep to these rules, and one draw needn't show every extreme that they name: `retrieved`: passage i lies on memory shard i // 16. Among the 12 ids of one device's questions, counting repeats, at most 2 lie on any one shard, and every device has 2 on some shard.
All inputs are finite; a program needn't handle non-finite values.
Results may differ from a plain program's by a relative error of at most 0.0075.
Values may be sent and summed in bfloat16 or wider, within the bound.
No kernel may reach another device: no remote copies, remote signals or barrier semaphores. Data moves between devices by JAX's collectives and lax.ppermute only.
A program may use at most 192 MiB of HBM per device.

v0:
```python
import math

import jax
import jax.numpy as jnp
from jax import lax
from jax.sharding import PartitionSpec as P

HS = 64
CAPM = 2


def normalize(rows, norm_gain):
    widened = rows.astype(jnp.float32)
    scale_sq = jnp.mean(widened * widened, axis=-1, keepdims=True)
    return (widened * lax.rsqrt(scale_sq + 1e-06) * norm_gain.astype(jnp.float32)).astype(
        jnp.bfloat16
    )


def body(questions, memory, retrieved, q_len, p_len, norm_gain, w_query, w_key, w_value, w_out):
    shards = lax.axis_size("mem")
    quest_dev, q_tokens, half_width = questions.shape
    pass_dev, p_tokens, _ = memory.shape
    per_question = retrieved.shape[1]
    pair_count = quest_dev * per_question
    capacity = CAPM
    wanted = retrieved.reshape(pair_count)
    shard_of = wanted // pass_dev
    local_id = wanted - shard_of * pass_dev
    pair_index = jnp.arange(pair_count, dtype=jnp.int32)
    before = (shard_of[:, None] == shard_of[None, :]) & (pair_index[None, :] < pair_index[:, None])
    rank_same = jnp.sum(before.astype(jnp.int32), axis=1)
    peer_ids = jnp.arange(shards, dtype=jnp.int32)
    places = jnp.arange(capacity, dtype=jnp.int32)
    chosen = (shard_of[None, None, :] == peer_ids[:, None, None]) & (
        rank_same[None, None, :] == places[None, :, None]
    )
    request_table = jnp.sum(jnp.where(chosen, local_id[None, None, :] + 1, 0), axis=2) - 1
    requested = lax.all_to_all(request_table, "mem", split_axis=0, concat_axis=0, tiled=True)
    all_lengths = lax.all_gather(p_len, "mem", axis=0, tiled=True)
    pair_plen = all_lengths[wanted]
    pair_qlen = jnp.repeat(q_len, per_question)
    fetch_index = shard_of * capacity + rank_same
    full_memory, full_questions = (
        lax.all_gather(memory, "tp", axis=2, tiled=True),
        lax.all_gather(questions, "tp", axis=2, tiled=True),
    )
    full_width = full_memory.shape[2]
    picked = full_memory[jnp.maximum(requested, 0)]
    arrived = lax.all_to_all(
        jnp.where((requested >= 0)[:, :, None, None], picked, jnp.zeros_like(picked)),
        "mem",
        split_axis=0,
        concat_axis=0,
        tiled=True,
    )
    passage_rows = arrived.reshape(shards * capacity, p_tokens, full_width)[fetch_index]
    own_passages = lax.dynamic_slice_in_dim(
        passage_rows, lax.axis_index("tp") * half_width, half_width, 2
    )
    own_half = jnp.concatenate([jnp.repeat(questions, per_question, axis=0), own_passages], axis=1)
    total_len = q_tokens + p_tokens
    spots = jnp.arange(total_len, dtype=jnp.int32)[None, :]
    usable = jnp.where(
        spots < q_tokens, spots < pair_qlen[:, None], spots - q_tokens < pair_plen[:, None]
    )
    question_normed = normalize(full_questions, norm_gain).reshape(quest_dev * q_tokens, full_width)
    passage_normed = normalize(passage_rows, norm_gain).reshape(pair_count * p_tokens, full_width)
    heads_dev = w_query.shape[1] // HS

    def project(weight):
        made_q = jnp.dot(question_normed, weight, preferred_element_type=jnp.float32).astype(
            jnp.bfloat16
        )
        made_q = made_q.reshape(quest_dev, 1, q_tokens, heads_dev, HS)
        made_q = jnp.broadcast_to(made_q, (quest_dev, per_question, q_tokens, heads_dev, HS))
        made_q = made_q.reshape(pair_count, q_tokens, heads_dev, HS)
        made_p = jnp.dot(passage_normed, weight, preferred_element_type=jnp.float32).astype(
            jnp.bfloat16
        )
        made_p = made_p.reshape(pair_count, p_tokens, heads_dev, HS)
        return jnp.concatenate([made_q, made_p], axis=1)

    query_heads = project(w_query)
    key_heads = project(w_key)
    value_heads = project(w_value)
    scores = jnp.einsum(
        "pqhd,pkhd->phqk", query_heads, key_heads, preferred_element_type=jnp.float32
    )
    scores = scores * (1.0 / math.sqrt(HS))
    scores = jnp.where(usable[:, None, None, :], scores, -1e30)
    row_max = jnp.max(scores, axis=3, keepdims=True)
    raised = jnp.exp(scores - row_max)
    attention_weights = (raised / jnp.sum(raised, axis=3, keepdims=True)).astype(jnp.bfloat16)
    attended = jnp.einsum(
        "phqk,pkhd->pqhd", attention_weights, value_heads, preferred_element_type=jnp.float32
    )
    attended = attended.astype(jnp.bfloat16).reshape(pair_count * total_len, heads_dev * HS)
    partial_value = jnp.dot(attended, w_out, preferred_element_type=jnp.float32).reshape(
        pair_count, total_len, full_width
    )
    summed = lax.psum_scatter(
        partial_value.astype(jnp.bfloat16), "tp", scatter_dimension=2, tiled=True
    ).astype(jnp.float32)
    encoded = (
        (own_half.astype(jnp.float32) + summed) * usable[:, :, None].astype(jnp.float32)
    ).astype(jnp.bfloat16)
    return encoded.reshape(quest_dev, per_question, total_len, half_width)


def solution(mesh):
    in_specs = (
        P(("groups", "mem"), None, "tp"),
        P("mem", None, "tp"),
        P(("groups", "mem"), None),
        P(("groups", "mem")),
        P("mem"),
        P(),
        P(None, "tp"),
        P(None, "tp"),
        P(None, "tp"),
        P("tp", None),
    )
    out_specs = P(("groups", "mem"), None, None, "tp")
    return jax.shard_map(body, mesh=mesh, in_specs=in_specs, out_specs=out_specs, check_vma=False)
```

profile of v0, /device:TPU:11, one launch (start us, length us, event | category | flops | bytes accessed | tf_op | source)
XLA Modules:
  0.0 441.1 jit_solution(6717716941696076657)
XLA Ops:
  9.0 9.6 %all_to_all.11 = s32[8,1,2]{2,1,0:T(1,128)S(1)} all-to-all(s32[8,1,2]{2,1,0:T(1,128)S(1)} %copy.48), channel_id=1, replica_groups=mesh['groups'=2,'mem'=8,'tp'=2] {'mem'}, dimensions={0} | all-to-all | bytes 128 | tf_op jit(solution)/shard_map/all_to_all | solution.py:39
  19.0 11.7 %all-gather.2.cloned.1.call-done = bf16[16,128,2048]{2,1,0:T(8,128)(2,1)} async-done(((bf16[16,128,1024]{2,1,0:T(8,128)(2,1)}), bf16[16,128,2048]{2,1,0:T(8,128)(2,1)}) %all-gather.2.cloned.1.call-update) | async-done | bytes 8388624 | tf_op jit(solution)/shard_map/all_gather | solution.py:45
  30.7 8.1 %gather_fusion = bf16[16,128,2048]{2,1,0:T(8,128)(2,1)} fusion(bf16[16,128,2048]{2,1,0:T(8,128)(2,1)} %all-gather.2.cloned.1.call-done, s32[1024]{0:T(1024)S(1)} %pad_clamp_fusion.2), kind=kCustom, calls=%fused_computation | custom fusion | bytes 16777280 | tf_op jit(solution)/shard_map/gather | solution.py:49
  38.8 7.2 %broadcast_select_fusion = bf16[8,2,128,2048]{3,2,1,0:T(8,128)(2,1)} fusion(bf16[8,2,128,2048]{3,2,1,0:T(8,128)(2,1)} %bitcast.76, pred[8,2]{1,0:T(8,128)(4,1)S(1)} %copy.50), kind=kLoop, calls=%fused_computation.16 | loop fusion | flops 4194304 | bytes 16777232 | tf_op jit(solution)/shard_map/jit(_where)/select_n | solution.py:51
  46.0 5.6 %all-to-all-start.1 = ((bf16[8,2,128,2048]{3,2,1,0:T(8,128)(2,1)}), bf16[8,2,128,2048]{3,2,1,0:T(8,128)(2,1)}, u32[]{:S(2)}, u32[]{:S(2)}) async-start(bf16[8,2,128,2048]{3,2,1,0:T(8,128)(2,1)} %broadcast_select_fusion), calls=%async_computation.1 | async-start | bytes 16777216 | tf_op jit(solution)/shard_map/all_to_all | solution.py:50
  52.3 2.3 all_gather.10
  54.8 3.1 convolution_convert_fusion.6
  58.1 3.1 convolution_convert_fusion.4
  62.0 3.1 convolution_convert_fusion.5
  65.0 0.8 copy.67
  67.4 165.8 %all-reduce = s32[128]{0:T(128)S(1)} all-reduce(s32[128]{0:T(128)S(1)} %dynamic-update-slice), channel_id=1, replica_groups=mesh['groups'=2,'mem'=8,'tp'=2] {'mem'}, use_global_device_ids=true, to_apply=%add | all-reduce | flops 128 | bytes 1024
  234.6 7.5 %gather_fusion.1 = bf16[12,128,2048]{2,1,0:T(8,128)(2,1)} fusion(bf16[16,128,2048]{2,1,0:T(8,128)(2,1)} %bitcast.6, s32[1024]{0:T(1024)S(1)} %pad_clamp_fusion.1), kind=kCustom, calls=%fused_computation.1 | custom fusion | bytes 12582960 | tf_op jit(solution)/shard_map/gather | solution.py:57
  242.1 4.2 multiply_reduce_fusion
  246.7 1.5 fusion.7
  248.9 8.0 %convolution_convert_fusion.1 = bf16[1536,1024]{1,0:T(8,128)(2,1)} fusion(bf16[1536,2048]{1,0:T(8,128)(2,1)S(1)} %fusion.7, bf16[2048,1024]{1,0:T(8,128)(2,1)S(1)} %copy-done.1), kind=kOutput, calls=%fused_computation.31 | convolution fusion | flops 6444023808 | bytes 13631488 | tf_op jit(solution)/shard_map/dot_general | solution.py:78
  256.9 8.0 %convolution_convert_fusion.2 = bf16[1536,1024]{1,0:T(8,128)(2,1)} fusion(bf16[1536,2048]{1,0:T(8,128)(2,1)S(1)} %fusion.7, bf16[2048,1024]{1,0:T(8,128)(2,1)S(1)} %copy-done.2), kind=kOutput, calls=%fused_computation.32 | convolution fusion | flops 6444023808 | bytes 13631488 | tf_op jit(solution)/shard_map/dot_general | solution.py:78
  265.0 8.1 %convolution_convert_fusion.3 = bf16[1536,1024]{1,0:T(8,128)(2,1)} fusion(bf16[1536,2048]{1,0:T(8,128)(2,1)S(1)} %fusion.7, bf16[2048,1024]{1,0:T(8,128)(2,1)S(1)} %copy-done.3), kind=kOutput, calls=%fused_computation.33 | convolution fusion | flops 6444023808 | bytes 13631488 | tf_op jit(solution)/shard_map/dot_general | solution.py:78
  273.1 6.1 %reshape.484 = bf16[12,128,16,64]{3,2,1,0:T(8,128)(2,1)} reshape(bf16[1536,1024]{1,0:T(8,128)(2,1)S(1)} %copy-done.4) | data formatting | bytes 6291456 | tf_op jit(solution)/shard_map/reshape | solution.py:81
  279.2 7.2 %copy.59 = bf16[12,128,16,64]{1,3,2,0:T(8,128)(2,1)S(1)} copy(bf16[12,128,16,64]{3,2,1,0:T(8,128)(2,1)} %reshape.484) | data formatting | bytes 6291456 | tf_op jit(solution)/shard_map/reshape | solution.py:81
  286.4 9.2 %reshape.482 = bf16[12,128,16,64]{3,2,1,0:T(8,128)(2,1)} reshape(bf16[1536,1024]{1,0:T(8,128)(2,1)} %convolution_convert_fusion.3) | data formatting | bytes 6291456 | tf_op jit(solution)/shard_map/reshape | solution.py:81
  295.6 8.0 %copy.53 = bf16[12,128,16,64]{1,3,2,0:T(8,128)(2,1)} copy(bf16[12,128,16,64]{3,2,1,0:T(8,128)(2,1)} %reshape.482) | data formatting | bytes 6291456 | tf_op jit(solution)/shard_map/reshape | solution.py:81
  303.6 9.2 %reshape.483 = bf16[12,128,16,64]{3,2,1,0:T(8,128)(2,1)} reshape(bf16[1536,1024]{1,0:T(8,128)(2,1)} %convolution_convert_fusion.2) | data formatting | bytes 6291456 | tf_op jit(solution)/shard_map/reshape | solution.py:81
  312.8 8.0 %copy.56 = bf16[12,128,16,64]{1,3,2,0:T(8,128)(2,1)} copy(bf16[12,128,16,64]{3,2,1,0:T(8,128)(2,1)} %reshape.483) | data formatting | bytes 6291456 | tf_op jit(solution)/shard_map/reshape | solution.py:81
  320.9 3.4 reshape.444
  324.2 3.5 reshape.446
  327.7 17.0 %fusion.11 = f32[12,16,160,160]{2,3,1,0:T(8,128)} fusion(bf16[12,128,16,64]{1,3,2,0:T(8,128)(2,1)} %copy.56, bf16[12,32,16,64]{1,3,2,0:T(8,128)(2,1)} %reshape.444, bf16[12,128,16,64]{1,3,2,0:T(8,128)(2,1)S(1)} %copy.59, bf16[12,32,16,64]{1,3,2,0:T(8,128)(2,1)} %reshape.446), kind=kOutput, calls=%fused_computation.21 | convolution fusion | flops 644874240 | bytes 27525120 | tf_op jit(solution)/shard_map/pqhd,pkhd->phqk/dot_general | solution.py:87
  344.8 36.2 %fusion.41 = (f32[12,16,160]{2,1,0:T(8,128)}, f32[12,16,160,160]{2,3,1,0:T(8,128)}) fusion(f32[12,16,160,160]{2,3,1,0:T(8,128)} %fusion.11, pred[12,160]{1,0:T(8,128)(4,1)S(1)} %get-tuple-element.8), kind=kOutput, calls=%fused_computation.90 | output fusion | flops 29491360 | bytes 39446400 | tf_op jit(solution)/shard_map/sub | solution.py:93
  381.8 15.9 %fusion.20 = bf16[12,16,64,160]{3,2,1,0:T(8,128)(2,1)} fusion(f32[12,16,160,160]{2,3,1,0:T(8,128)} %get-tuple-element.12, f32[12,16,160]{2,1,0:T(8,128)} %get-tuple-element.11, bf16[12,128,16,64]{1,3,2,0:T(8,128)(2,1)} %copy.53, bf16[12,32,16,64]{1,3,2,0:T(8,128)(2,1)S(1)} %reshape.442), kind=kOutput, calls=%fused_computation.34 | convolution fusion | flops 648806400 | bytes 27648000 | tf_op jit(solution)/shard_map/phqk,pkhd->pqhd/dot_general | solution.py:95
  397.7 13.7 %convolution_convert_fusion = bf16[12,160,2048]{2,1,0:T(8,128)(2,1)} fusion(bf16[12,160,1024]{1,2,0:T(8,128)(2,1)} %bitcast.82, bf16[1024,2048]{1,0:T(8,128)(2,1)} %param.19), kind=kOutput, calls=%fused_computation.28 | convolution fusion | flops 8056995840 | bytes 15990784 | tf_op jit(solution)/shard_map/dot_general | solution.py:99
  411.4 2.5 constant_dynamic-slice_fusion
  413.8 15.9 %reduce-scatter.2.cloned.1.call-done = bf16[12,160,1024]{2,1,0:T(8,128)(2,1)} async-done(((bf16[12,160,2048]{2,1,0:T(8,128)(2,1)}), bf16[12,160,1024]{2,1,0:T(8,128)(2,1)}) %reduce-scatter.2.cloned.1.call-update) | async-done | bytes 3932176 | tf_op jit(solution)/shard_map/reduce_scatter | solution.py:102
  429.8 4.1 fusion.19
  (61 shorter events, 8.1 us)
Async XLA Ops:
  6.5 24.1 %all-gather.2.cloned.1.call-start = ((), (), s32[]{:S(2)}) async-start(), calls=%async_computation.3 | async-start | bytes 12582912 | tf_op jit(solution)/shard_map/all_gather | solution.py:45
  46.0 6.3 %copy-start.8 = (bf16[2048]{0:T(1024)(128)(2,1)S(1)}, bf16[2048]{0:T(1024)(128)(2,1)}, u32[]{:S(2)}) copy-start(bf16[2048]{0:T(1024)(128)(2,1)} %param.15) | copy-start | bytes 12292
  46.0 6.3 %copy-start.5 = (bf16[1,32,1024]{2,1,0:T(8,128)(2,1)S(1)}, bf16[1,32,1024]{2,1,0:T(8,128)(2,1)}, u32[]{:S(2)}) copy-start(bf16[1,32,1024]{2,1,0:T(8,128)(2,1)} %param.10) | copy-start | bytes 196612
  46.0 188.6 %all-to-all-start.1 = ((bf16[8,2,128,2048]{3,2,1,0:T(8,128)(2,1)}), bf16[8,2,128,2048]{3,2,1,0:T(8,128)(2,1)}, u32[]{:S(2)}, u32[]{:S(2)}) async-start(bf16[8,2,128,2048]{3,2,1,0:T(8,128)(2,1)} %broadcast_select_fusion), calls=%async_computation.1 | async-start | bytes 16777216 | tf_op jit(solution)/shard_map/all_to_all | solution.py:50
  51.6 378.1 %reduce-scatter.2.cloned.1.call-start = ((), (), s32[]{:S(2)}) async-start(), calls=%async_computation.4 | async-start | bytes 11796480 | tf_op jit(solution)/shard_map/reduce_scatter | solution.py:102
  54.8 11.1 %copy-start.11 = (u32[32]{0:T(128)S(1)}, u32[32]{0:T(128)}, u32[]{:S(2)}) copy-start(u32[32]{0:T(128)} %constant.65) | copy-start | bytes 388
  54.8 12.3 %copy-start.10 = (s32[16]{0:T(128)S(1)}, s32[16]{0:T(128)}, u32[]{:S(2)}) copy-start(s32[16]{0:T(128)} %param.14) | copy-start | bytes 196
  54.8 178.4 %copy-start.9 = (s32[1,12]{1,0:T(1,128)S(1)}, s32[1,12]{1,0:T(1,128)}, u32[]{:S(2)}) copy-start(s32[1,12]{1,0:T(1,128)} %param.12) | copy-start | bytes 148
  242.1 4.6 %copy-start = (bf16[12,128,2048]{2,1,0:T(8,128)(2,1)S(1)}, bf16[12,128,2048]{2,1,0:T(8,128)(2,1)}, u32[]{:S(2)}) copy-start(bf16[12,128,2048]{2,1,0:T(8,128)(2,1)} %gather_fusion.1) | copy-start | bytes 18874372
  246.7 2.2 copy-start.1
  248.9 8.0 %copy-start.2 = (bf16[2048,1024]{1,0:T(8,128)(2,1)S(1)}, bf16[2048,1024]{1,0:T(8,128)(2,1)}, u32[]{:S(2)}) copy-start(bf16[2048,1024]{1,0:T(8,128)(2,1)} %param.16) | copy-start | bytes 12582916
  256.9 8.0 %copy-start.3 = (bf16[2048,1024]{1,0:T(8,128)(2,1)S(1)}, bf16[2048,1024]{1,0:T(8,128)(2,1)}, u32[]{:S(2)}) copy-start(bf16[2048,1024]{1,0:T(8,128)(2,1)} %param.18) | copy-start | bytes 12582916
  265.0 8.1 %copy-start.4 = (bf16[1536,1024]{1,0:T(8,128)(2,1)S(1)}, bf16[1536,1024]{1,0:T(8,128)(2,1)}, u32[]{:S(2)}) copy-start(bf16[1536,1024]{1,0:T(8,128)(2,1)} %convolution_convert_fusion.1) | copy-start | bytes 9437188
  411.3 18.4 %copy-start.6 = (bf16[1,32,1024]{2,1,0:T(8,128)(2,1)S(1)}, bf16[1,32,1024]{2,1,0:T(8,128)(2,1)}, u32[]{:S(2)}) copy-start(bf16[1,32,1024]{2,1,0:T(8,128)(2,1)} %param.10) | copy-start | bytes 196612
  411.3 18.4 %copy-start.7 = (f32[12,160]{1,0:T(8,128)S(1)}, f32[12,160]{1,0:T(8,128)}, u32[]{:S(2)}) copy-start(f32[12,160]{1,0:T(8,128)} %get-tuple-element.7) | copy-start | bytes 23044
Sparse Core Ops, SparseCore 0:
  8.9 21.7 all-gather.1
  411.5 18.1 reduce-scatter.1
where the time goes:
time: 447 us; the launch traced here: 441 us
  blocking collectives  178 us (40%)
  matrix products  79.9 us (18%)
  local copies, waits for them, and re-layouts  78.4 us (18%)
  other arithmetic  55.8 us (12%)
  waiting for transfers between devices  28.3 us (6%)
  between operations  15.3 us (3%)
  starting transfers between devices  5.63 us (1%)
    unnamed x1, blocking collectives  166 us
    reshape x6, local copies, waits for them, and re-layouts, project(): made_p = made_p.reshape(pair_count, p_tokens, heads_dev, HS)  47.8 us
    sub x1, other arithmetic, body(): raised = jnp.exp(scores - row_max)  36.2 us
    dot_general x3, matrix products, project(): jnp.dot(passage_normed, weight, preferred_element_type=jnp.float32)  24.1 us
    dot_general x1, matrix products, body(): jnp.einsum('pqhd,pkhd->phqk', query_heads, key_heads, preferred_element_t...  17 us
    dot_general x1, matrix products, body(): jnp.einsum('phqk,pkhd->pqhd', attention_weights, value_heads, preferred_e...  15.9 us
    reduce_scatter x1, waiting for transfers between devices, body(): lax.psum_scatter(partial_value.astype(jnp.bfloat16), 'tp', scatter_dimens...  15.9 us
    dot_general x1, matrix products, body(): jnp.dot(attended, w_out, preferred_element_type=jnp.float32)  13.7 us
  transfers between devices with their start and end apart: 3, of which 2 were waited for; matrix products, arithmetic and copies ran while one was open for 4% of the time, Pallas kernels for 0%

commit v1 on v0

v1 whole, which is shorter than its diff:
```python
import functools

import jax
import jax.numpy as jnp
from jax import lax
from jax.experimental import pallas as pl
from jax.experimental.pallas import tpu as pltpu
from jax.sharding import PartitionSpec as P

HS = 64
CAPM = 2
EPS = 1e-06
MASKED = -1e30
LANES = 128
VMEM_LIMIT = 56 * 1024 * 1024

ANY = pl.BlockSpec(memory_space=pl.ANY)
SMEM = pl.BlockSpec(memory_space=pltpu.SMEM)
VMEM = pl.BlockSpec(memory_space=pltpu.VMEM)


def pick_kernel(shards, pass_dev, wants, own_ref, *refs):
    metas = refs[:shards]
    memory = refs[shards]
    outs = refs[shards + 1 : 2 * shards + 1]
    table = refs[2 * shards + 1]
    sems = refs[2 * shards + 2]
    me = own_ref[0, 1]
    low = me * pass_dev
    counts = []
    for k in range(shards):

        def ask(j, count):
            local = metas[k][0, j] - low
            mine = jnp.logical_and(local >= 0, local < pass_dev)

            @pl.when(mine)
            def _():
                pltpu.make_async_copy(
                    memory.at[local], outs[k].at[count], sems.at[k, count]
                ).start()

            return count + mine.astype(jnp.int32)

        counts.append(lax.fori_loop(0, wants, ask, jnp.int32(0)))
    for k in range(shards):
        partner_low = lax.bitwise_xor(me, k) * pass_dev
        for r in range(CAPM):
            table[0, CAPM * k + r] = jnp.int32(-1)
            table[1, CAPM * k + r] = jnp.int32(0)

        def place(j, count):
            local = metas[0][0, j] - partner_low
            theirs = jnp.logical_and(local >= 0, local < pass_dev)

            @pl.when(theirs)
            def _():
                table[0, CAPM * k + count] = j
                table[1, CAPM * k + count] = metas[k][0, wants + local]

            return count + theirs.astype(jnp.int32)

        lax.fori_loop(0, wants, place, jnp.int32(0))
    for k in range(shards):
        for r in range(CAPM):

            @pl.when(r < counts[k])
            def _():
                pltpu.make_async_copy(memory.at[0], outs[k].at[r], sems.at[k, r]).wait()


def pick(own, metas, memory, wants):
    shards = len(metas)
    pass_dev, p_tokens, half = memory.shape
    slot = jax.ShapeDtypeStruct((CAPM, p_tokens, half), memory.dtype)
    result = pl.pallas_call(
        functools.partial(pick_kernel, shards, pass_dev, wants),
        out_shape=[slot] * shards + [jax.ShapeDtypeStruct((2, LANES), jnp.int32)],
        in_specs=[SMEM] * (shards + 1) + [ANY],
        out_specs=[ANY] * shards + [SMEM],
        scratch_shapes=[pltpu.SemaphoreType.DMA((shards, CAPM))],
        cost_estimate=pl.CostEstimate(
            flops=0, bytes_accessed=2 * shards * CAPM * p_tokens * half * 2, transcendentals=0
        ),
        name="pick",
    )(own, *metas, memory)
    return result[:shards], result[shards]


def normed_halves(own, other, gain_own, gain_other):
    own = own.astype(jnp.float32)
    other = other.astype(jnp.float32)
    total = jnp.sum(own * own + other * other, axis=-1, keepdims=True)
    scale = lax.rsqrt(total / (2 * own.shape[-1]) + EPS)
    return (
        (own * scale * gain_own).astype(jnp.bfloat16),
        (other * scale * gain_other).astype(jnp.bfloat16),
    )


def weight_copies(c, half, sources, targets, sems):
    copies = []
    for i, (source, target) in enumerate(zip(sources, targets)):
        pieces = []
        for part, core in enumerate((c, 1 - c)):
            start = pl.multiple_of(core * half, half)
            pieces.append(
                pltpu.make_async_copy(
                    source.at[pl.ds(start, half), :],
                    target.at[pl.ds(part * half, half), :],
                    sems.at[i, part],
                )
            )
        copies.append(pieces)
    return copies


def question_kernel(own_ref, mine, theirs, gain, wq, wk, wv, out, vq, vk, vv, sems):
    c = own_ref[0, 0]
    half = mine.shape[-1]
    copies = weight_copies(c, half, (wq, wk, wv), (vq, vk, vv), sems)
    for pieces in copies:
        for piece in pieces:
            piece.start()
    g_own = gain[c].astype(jnp.float32)
    g_other = gain[1 - c].astype(jnp.float32)
    first, second = normed_halves(mine[0], theirs[0], g_own, g_other)
    rows = jnp.concatenate([first, second], axis=1)
    for i, weight in enumerate((vq, vk, vv)):
        for piece in copies[i]:
            piece.wait()
        made = jnp.dot(rows, weight[...], preferred_element_type=jnp.float32)
        made = made.astype(jnp.bfloat16)
        if i == 0:
            made = made * jnp.bfloat16(1.0 / 8.0)
        out[i] = made


def project_question(own, mine, theirs, gain, wq, wk, wv):
    _, q_tokens, half = mine.shape
    width, cols = wq.shape
    weight = pltpu.VMEM((width, cols), jnp.bfloat16)
    return pl.pallas_call(
        question_kernel,
        out_shape=jax.ShapeDtypeStruct((3, q_tokens, cols), jnp.bfloat16),
        in_specs=[SMEM, VMEM, VMEM, VMEM, ANY, ANY, ANY],
        out_specs=VMEM,
        scratch_shapes=[weight] * 3 + [pltpu.SemaphoreType.DMA((3, 2))],
        compiler_params=pltpu.CompilerParams(vmem_limit_bytes=VMEM_LIMIT),
        cost_estimate=pl.CostEstimate(
            flops=6 * q_tokens * width * cols, bytes_accessed=6 * width * cols, transcendentals=0
        ),
        name="question_projections",
    )(own, mine, theirs, gain, wq, wk, wv)


def layer_kernel(ks, own_ref, table, question, gain, *refs):
    n = len(ks)
    mine, theirs = refs[:n], refs[n : 2 * n]
    wq, wk, wv, wo = refs[2 * n : 2 * n + 4]
    out_own, out_other = refs[2 * n + 4 : 2 * n + 6]
    vq, vk, vv, vo, rows, query, key, value, attended, sems, sems_out = refs[2 * n + 6 :]
    slots, total, cols = query.shape
    q_tokens = question.shape[1]
    p_tokens = total - q_tokens
    half = mine[0].shape[-1]
    c = own_ref[0, 0]
    q_len = own_ref[0, 2]
    copies = weight_copies(c, half, (wq, wk, wv), (vq, vk, vv), sems)
    out_copies = []
    for part, core in enumerate((1 - c, c)):
        start = pl.multiple_of(core * half, half)
        out_copies.append(
            pltpu.make_async_copy(wo.at[:, pl.ds(start, half)], vo.at[part], sems_out.at[part])
        )
    for pieces in copies + [out_copies]:
        for piece in pieces:
            piece.start()
    g_own = gain[c].astype(jnp.float32)
    g_other = gain[1 - c].astype(jnp.float32)
    for i in range(n):
        for r in range(CAPM):
            first, second = normed_halves(mine[i][r], theirs[i][r], g_own, g_other)
            at = pl.ds((CAPM * i + r) * p_tokens, p_tokens)
            rows[at, :half] = first
            rows[at, half:] = second
    for i, (weight, target) in enumerate(((vq, query), (vk, key), (vv, value))):
        for piece in copies[i]:
            piece.wait()
        for s in range(slots):
            target[s, :q_tokens, :] = question[i]
        for left in range(0, cols, 256):
            span = slice(left, left + 256)
            made = jnp.dot(rows[...], weight[:, span], preferred_element_type=jnp.float32)
            made = made.astype(jnp.bfloat16)
            if i == 0:
                made = made * jnp.bfloat16(1.0 / 8.0)
            for s in range(slots):
                target[s, q_tokens:, span] = made[s * p_tokens : (s + 1) * p_tokens]

    lane = lax.broadcasted_iota(jnp.int32, (1, 2 * HS), 1)
    in_first = lane < HS
    spot = lax.broadcasted_iota(jnp.int32, (1, total), 1)
    ones = jnp.ones((total, 2 * HS), jnp.bfloat16)

    def attend(s, carry):
        slot = CAPM * ks[0] + s
        p_len = table[1, slot]

        @pl.when(p_len > 0)
        def _():
            end = jnp.where(spot < q_tokens, q_len, q_tokens + p_len)
            bias = jnp.where(spot < end, 0.0, MASKED)
            for left in range(0, cols, 2 * HS):
                span = slice(left, left + 2 * HS)
                q2 = query[s, :, span]
                zero = jnp.zeros_like(q2)
                q2 = jnp.concatenate(
                    [jnp.where(in_first, q2, zero), jnp.where(in_first, zero, q2)], axis=0
                )
                scores = lax.dot_general(
                    q2,
                    key[s, :, span],
                    (((1,), (1,)), ((), ())),
                    preferred_element_type=jnp.float32,
                )
                scores = scores + bias
                raised = jnp.exp(scores - jnp.max(scores, axis=1, keepdims=True))
                with_sum = jnp.dot(
                    raised.astype(jnp.bfloat16),
                    jnp.concatenate([value[s, :, span], ones], axis=1),
                    preferred_element_type=jnp.float32,
                )
                mixed = with_sum[:, : 2 * HS] / with_sum[:, 2 * HS :]
                attended[s, :, span] = jnp.where(
                    in_first, mixed[:total], mixed[total:]
                ).astype(jnp.bfloat16)

        return carry

    lax.fori_loop(0, slots, attend, 0)
    for part, out in enumerate((out_other, out_own)):
        out_copies[part].wait()
        flat = attended[...].reshape(slots * total, cols)
        for left in range(0, half, 256):
            span = slice(left, left + 256)
            made = jnp.dot(flat, vo[part, :, span], preferred_element_type=jnp.float32)
            out[:, :, span] = made.astype(jnp.bfloat16).reshape(slots, total, 256)


def layer(ks, own, table, question, gain, mine, theirs, wq, wk, wv, wo):
    _, p_tokens, half = mine[0].shape
    _, q_tokens, cols = question.shape
    width = wq.shape[0]
    slots = CAPM * len(ks)
    total = q_tokens + p_tokens
    weight = pltpu.VMEM((width, cols), jnp.bfloat16)
    split = pltpu.VMEM((slots, total, cols), jnp.bfloat16)
    out = jax.ShapeDtypeStruct((slots, total, half), jnp.bfloat16)
    return pl.pallas_call(
        functools.partial(layer_kernel, ks),
        out_shape=[out, out],
        in_specs=[SMEM, SMEM, VMEM, VMEM] + [VMEM] * (2 * len(ks)) + [ANY] * 4,
        out_specs=[VMEM, VMEM],
        scratch_shapes=[weight] * 3
        + [
            pltpu.VMEM((2, cols, half), jnp.bfloat16),
            pltpu.VMEM((slots * p_tokens, width), jnp.bfloat16),
            split,
            split,
            split,
            split,
            pltpu.SemaphoreType.DMA((3, 2)),
            pltpu.SemaphoreType.DMA((2,)),
        ],
        compiler_params=pltpu.CompilerParams(vmem_limit_bytes=VMEM_LIMIT),
        cost_estimate=pl.CostEstimate(
            flops=slots * (6 * p_tokens * width * cols + 4 * total * cols * half),
            bytes_accessed=8 * width * cols,
            transcendentals=slots * total * total * cols // HS,
        ),
        name="layer",
    )(own, table, question, gain, *mine, *theirs, wq, wk, wv, wo)


def combine_kernel(ks, first, own_ref, table, questions, *refs):
    n = len(ks)
    mine = refs[:n]
    ours, arrived = refs[n : n + 2]
    encoded, staged, sems = refs[n + 2 if first else n + 3 :]
    slots, total, _ = ours.shape
    q_tokens = questions.shape[1]
    q_len = own_ref[0, 2]

    def copy(s, pair):
        return pltpu.make_async_copy(staged.at[s], encoded.at[0, pair], sems.at[s])

    for s in range(slots):
        pair = table[0, CAPM * ks[0] + s]
        p_len = table[1, CAPM * ks[0] + s]

        @pl.when(pair >= 0)
        def _():
            for rows, at, length in (
                (questions[0], slice(0, q_tokens), q_len),
                (mine[s // CAPM][s % CAPM], slice(q_tokens, total), p_len),
            ):
                spot = lax.broadcasted_iota(jnp.int32, (rows.shape[0], 1), 0)
                branch = ours[s, at].astype(jnp.float32) + arrived[s, at].astype(jnp.float32)
                made = rows.astype(jnp.float32) + branch
                staged[s, at] = jnp.where(spot < length, made, 0.0).astype(jnp.bfloat16)
            copy(s, pair).start()

    for s in range(slots):

        @pl.when(table[0, CAPM * ks[0] + s] >= 0)
        def _():
            copy(s, 0).wait()


def combine(ks, encoded, shape, own, table, questions, mine, ours, arrived):
    first = encoded is None
    operands = [own, table, questions, *mine, ours, arrived] + ([] if first else [encoded])
    return pl.pallas_call(
        functools.partial(combine_kernel, ks, first),
        out_shape=jax.ShapeDtypeStruct(shape, jnp.bfloat16),
        in_specs=[SMEM, SMEM, VMEM] + [VMEM] * (len(ks) + 2) + ([] if first else [ANY]),
        out_specs=ANY,
        scratch_shapes=[
            pltpu.VMEM(ours.shape, jnp.bfloat16),
            pltpu.SemaphoreType.DMA((ours.shape[0],)),
        ],
        input_output_aliases={} if first else {len(operands) - 1: 0},
        compiler_params=pltpu.CompilerParams(vmem_limit_bytes=VMEM_LIMIT),
        cost_estimate=pl.CostEstimate(
            flops=0, bytes_accessed=8 * ours.size, transcendentals=0
        ),
        name="combine",
    )(*operands)


def body(questions, memory, retrieved, q_len, p_len, norm_gain, w_query, w_key, w_value, w_out):
    shards = lax.axis_size("mem")
    cores = lax.axis_size("tp")
    _, q_tokens, half = questions.shape
    pass_dev, p_tokens, _ = memory.shape
    wants = retrieved.shape[1]

    def swap(x):
        return lax.ppermute(x, "tp", [(i, (i + 1) % cores) for i in range(cores)])

    def exchange(x, k):
        return lax.ppermute(x, "mem", [(i, i ^ k) for i in range(shards)])

    meta = jnp.concatenate(
        [retrieved[0], p_len, jnp.zeros((LANES - wants - pass_dev,), jnp.int32)]
    )[None]
    metas = [meta] + [exchange(meta, k) for k in range(1, shards)]
    own = jnp.concatenate(
        [
            lax.axis_index("tp").astype(jnp.int32)[None],
            lax.axis_index("mem").astype(jnp.int32)[None],
            q_len,
            jnp.zeros((LANES - 3,), jnp.int32),
        ]
    )[None]
    gain = norm_gain.reshape(cores, 1, half)
    question = project_question(
        own, questions, swap(questions), gain, w_query, w_key, w_value
    )
    sends, table = pick(own, metas, memory, wants)
    mine = [sends[0]] + [exchange(sends[k], k) for k in range(1, shards)]
    encoded = None
    shape = (1, wants, q_tokens + p_tokens, half)
    for low in range(0, shards, 2):
        ks = tuple(range(low, low + 2))
        rows = [mine[k] for k in ks]
        theirs = [swap(x) for x in rows]
        ours, other = layer(
            ks, own, table, question, gain, rows, theirs, w_query, w_key, w_value, w_out
        )
        encoded = combine(ks, encoded, shape, own, table, questions, rows, ours, swap(other))
    return encoded


def solution(mesh):
    in_specs = (
        P(("groups", "mem"), None, "tp"),
        P("mem", None, "tp"),
        P(("groups", "mem"), None),
        P(("groups", "mem")),
        P("mem"),
        P(),
        P(None, "tp"),
        P(None, "tp"),
        P(None, "tp"),
        P("tp", None),
    )
    out_specs = P(("groups", "mem"), None, None, "tp")
    return jax.shard_map(body, mesh=mesh, in_specs=in_specs, out_specs=out_specs, check_vma=False)
```

time: 447 us -> 323 us (0.72); the launches traced: 441 us -> 323 us
  Pallas kernels: 0 us -> 210 us
  blocking collectives: 178 us -> 0 us
  matrix products: 79.9 us -> 0 us
  local copies, waits for them, and re-layouts: 78.4 us -> 9.49 us
  other arithmetic: 55.8 us -> 1.34 us
  starting transfers between devices: 5.63 us -> 46.4 us
  waiting for transfers between devices: 28.3 us -> 54.3 us
  between operations: 15.3 us -> 1.5 us
    pallas_call x0 -> x10, Pallas kernels: none -> 210 us  [the longest x1 114 us: pick(): pl.pallas_call(functools.partial(pick_kernel, shards, pass_dev, wants), o...]
    unnamed x1 -> x0, blocking collectives: 166 us -> none
    dot_general x9 -> x0, matrix products: 79.9 us -> none  [the longest x3 24.1 us: project(): jnp.dot(passage_normed, weight, preferred_element_type=jnp.float32)]
    reshape x10 -> x1, local copies, waits for them, and re-layouts: 55.5 us -> 0.6 us  [body(): gain = norm_gain.reshape(cores, 1, half)]
    ppermute x0 -> x27, waiting for transfers between devices: none -> 54.3 us  [the longest x14 54.2 us: exchange(): return lax.ppermute(x, 'mem', [(i, i ^ k) for i in range(shards)])]
    ppermute x0 -> x27, starting transfers between devices: none -> 46.4 us  [the longest x14 35.7 us: exchange(): return lax.ppermute(x, 'mem', [(i, i ^ k) for i in range(shards)])]
    sub x3 -> x0, other arithmetic: 36.3 us -> none  [the longest x1 36.2 us: body(): raised = jnp.exp(scores - row_max)]
    gather x3 -> x0, local copies, waits for them, and re-layouts: 16.3 us -> none  [the longest x1 8.14 us: body(): picked = full_memory[jnp.maximum(requested, 0)]]
  transfers between devices with their start and end apart: 3 -> 27, of which waited for: 2 -> 7; matrix products, arithmetic and copies ran while one was open for 4% -> 0% of each run, Pallas kernels for 0% -> 29%
where the time goes in v1:
time: 323 us
  Pallas kernels  210 us (65%)
  waiting for transfers between devices  54.3 us (17%)
  starting transfers between devices  46.4 us (14%)
  local copies, waits for them, and re-layouts  9.49 us (3%)
    pallas_call x1, Pallas kernels, pick(): pl.pallas_call(functools.partial(pick_kernel, shards, pass_dev, wants), o...  114 us
    pallas_call x4, Pallas kernels, layer(): pl.pallas_call(functools.partial(layer_kernel, ks), out_shape=[out, out],...  76.2 us
    ppermute x14, waiting for transfers between devices, exchange(): return lax.ppermute(x, 'mem', [(i, i ^ k) for i in range(shards)])  54.2 us
    ppermute x14, starting transfers between devices, exchange(): return lax.ppermute(x, 'mem', [(i, i ^ k) for i in range(shards)])  35.7 us
    pallas_call x4, Pallas kernels, combine(): pl.pallas_call(functools.partial(combine_kernel, ks, first), out_shape=ja...  13.1 us
    ppermute x13, starting transfers between devices, swap(): return lax.ppermute(x, 'tp', [(i, (i + 1) % cores) for i in range(cores)])  10.7 us
    unnamed x66, local copies, waits for them, and re-layouts  8.88 us
    pallas_call x1, Pallas kernels, project_question(): pl.pallas_call(question_kernel, out_shape=jax.ShapeDtypeStruct((3, q_toke...  7.22 us
  transfers between devices with their start and end apart: 27, of which 7 were waited for; matrix products, arithmetic and copies ran while one was open for 0% of the time, Pallas kernels for 29%

profile of v1, /device:TPU:11, one launch (start us, length us, event | category | flops | bytes accessed | tf_op | source)
XLA Modules:
  0.0 323.3 jit_solution(11034395916438974926)
XLA Ops:
  0.8 1.2 collective-permute-start
  2.2 1.2 collective-permute-start.2
  3.4 2.3 collective-permute-start.3
  5.7 1.0 collective-permute-start.4
  7.4 1.4 collective-permute-start.5
  9.9 2.1 collective-permute-done.6.refs_7_
  12.6 113.8 %pick.1 = (bf16[2,128,1024]{2,1,0:T(8,128)(2,1)}, bf16[2,128,1024]{2,1,0:T(8,128)(2,1)}, bf16[2,128,1024]{2,1,0:T(8,128)(2,1)}, bf16[2,128,1024]{2,1,0:T(8,128)(...) custom-call(s32[1,128]{1,0:T(1,128)} %add_bitcast_fusion.own_ref, ...), custom_call_target="tpu_custom_call" | custom-call | bytes 8388608 | tf_op jit(solution)/shard_map/pick/pallas_call | solution.py:76
  126.5 3.6 %collective-permute-start.9 = (bf16[1,32,1024]{2,1,0:T(8,128)(2,1)S(1)}, bf16[1,32,1024]{2,1,0:T(8,128)(2,1)S(1)}, u32[]{:S(2)}, u32[]{:S(2)}) collective-permute-start(bf16[1,32,1024]{2,1,0:T(8,128)(2,1)S(1)} %copy-done), channel_id=1, source_target_pairs={{0,1},{1,0},{2,3},{3,2},{4,5},{5,4},{6,7},{7,6},{8,9},{9,8},{10,11... | collective-permute-start | bytes 196616 | tf_op jit(solution)/shard_map/ppermute | solution.py:350
  130.2 12.3 %collective-permute-start.18 = (bf16[2,128,1024]{2,1,0:T(8,128)(2,1)}, bf16[2,128,1024]{2,1,0:T(8,128)(2,1)S(1)}, u32[]{:S(2)}, u32[]{:S(2)}) collective-permute-start(bf16[2,128,1024]{2,1,0:T(8,128)(2,1)} %get-tuple-element.31), channel_id=1, source_target_pairs={{0,4},{2,6},{4,0},{6,2},{8,12},{10,14},{12,8},{14,10},{1,5},{3,7},... | collective-permute-start | bytes 1572872 | tf_op jit(solution)/shard_map/ppermute | solution.py:353
  144.0 7.2 %question_projections.1.question = bf16[3,32,1024]{2,1,0:T(8,128)(2,1)} custom-call(s32[1,128]{1,0:T(1,128)} %add_bitcast_fusion.own_ref, bf16[1,32,1024]{2,1,0:T(8,128)(2,1)} %questions.7, bf16[1,32,1024]{2,1,0:T(8,128)(2,1)} %copy-done.12, bf16[2,1,1024]{2,1,0:T(2,128)(2,1)} %reshape.4.gain, bf16[2048,1024]{1,0:T(8,128)(2,1)} %refs_4_.7, ...), custom_call_target="tpu_custom_call" | custom-call | flops 402653184 | bytes 12582912 | tf_op jit(solution)/shard_map/question_projections/pallas_call | solution.py:143
  151.3 3.4 %collective-permute-start.14 = (bf16[2,128,1024]{2,1,0:T(8,128)(2,1)S(1)}, bf16[2,128,1024]{2,1,0:T(8,128)(2,1)S(1)}, u32[]{:S(2)}, u32[]{:S(2)}) collective-permute-start(bf16[2,128,1024]{2,1,0:T(8,128)(2,1)S(1)} %copy-done.24), channel_id=1, source_target_pairs={{0,10},{2,8},{4,14},{6,12},{8,2},{10,0},{12,6},{14,4},{1,11},{3,9}... | collective-permute-start | bytes 1572872 | tf_op jit(solution)/shard_map/ppermute | solution.py:353
  154.7 10.6 %collective-permute-done.18.refs_0_ = bf16[2,128,1024]{2,1,0:T(8,128)(2,1)S(1)} collective-permute-done((bf16[2,128,1024]{2,1,0:T(8,128)(2,1)}, bf16[2,128,1024]{2,1,0:T(8,128)(2,1)S(1)}, u32[]{:S(2)}, u32[]{:S(2)}) %collective-permute-start.18) | collective-permute-done | bytes 524320 | tf_op jit(solution)/shard_map/ppermute | solution.py:353
  165.3 5.8 %collective-permute-start.7 = (bf16[2,128,1024]{2,1,0:T(8,128)(2,1)S(1)}, bf16[2,128,1024]{2,1,0:T(8,128)(2,1)S(1)}, u32[]{:S(2)}, u32[]{:S(2)}) collective-permute-start(bf16[2,128,1024]{2,1,0:T(8,128)(2,1)S(1)} %copy-done.23), channel_id=1, source_target_pairs={{0,12},{2,14},{4,8},{6,10},{8,4},{10,6},{12,0},{14,2},{1,13},{3,15... | collective-permute-start | bytes 1572872 | tf_op jit(solution)/shard_map/ppermute | solution.py:353
  171.1 5.4 %collective-permute-done.19.refs_1_ = bf16[2,128,1024]{2,1,0:T(8,128)(2,1)S(1)} collective-permute-done((bf16[2,128,1024]{2,1,0:T(8,128)(2,1)}, bf16[2,128,1024]{2,1,0:T(8,128)(2,1)S(1)}, u32[]{:S(2)}, u32[]{:S(2)}) %collective-permute-start.19) | collective-permute-done | bytes 524320 | tf_op jit(solution)/shard_map/ppermute | solution.py:353
  176.6 6.6 %collective-permute-start.8 = (bf16[2,128,1024]{2,1,0:T(8,128)(2,1)S(1)}, bf16[2,128,1024]{2,1,0:T(8,128)(2,1)S(1)}, u32[]{:S(2)}, u32[]{:S(2)}) collective-permute-start(bf16[2,128,1024]{2,1,0:T(8,128)(2,1)S(1)} %copy-done.22), channel_id=1, source_target_pairs={{0,14},{2,12},{4,10},{6,8},{8,6},{10,4},{12,2},{14,0},{1,15},{3,13... | collective-permute-start | bytes 1572872 | tf_op jit(solution)/shard_map/ppermute | solution.py:353
  183.1 1.3 collective-permute-start.20
  185.3 17.8 %layer.7 = (bf16[4,160,1024]{2,1,0:T(8,128)(2,1)}, bf16[4,160,1024]{2,1,0:T(8,128)(2,1)}) custom-call(s32[1,128]{1,0:T(1,128)} %add_bitcast_fusion.own_ref, s32[2,128]{1,0:T(2,128)} %get-tuple-element.22.table, bf16[3,32,1024]{2,1,0:T(8,128)(2,1)} %question_projections.1.question, bf16[2,1,1024]{2,1,0:T(2,128)(2,1)} %reshape.4.gain, ...), custom_call_target="tpu_custom_call" | custom-call | flops 9126805504 | bytes 16777216 | tf_op jit(solution)/shard_map/layer/pallas_call | solution.py:260
  203.1 7.7 %collective-permute-done.14.refs_1_ = bf16[2,128,1024]{2,1,0:T(8,128)(2,1)S(1)} collective-permute-done((bf16[2,128,1024]{2,1,0:T(8,128)(2,1)S(1)}, bf16[2,128,1024]{2,1,0:T(8,128)(2,1)S(1)}, u32[]{:S(2)}, u32[]{:S(2)}) %collective-permute-start.14) | collective-permute-done | bytes 524320 | tf_op jit(solution)/shard_map/ppermute | solution.py:353
  210.8 1.5 collective-permute-start.15
  212.3 17.7 %collective-permute-done.7.refs_0_ = bf16[2,128,1024]{2,1,0:T(8,128)(2,1)S(1)} collective-permute-done((bf16[2,128,1024]{2,1,0:T(8,128)(2,1)S(1)}, bf16[2,128,1024]{2,1,0:T(8,128)(2,1)S(1)}, u32[]{:S(2)}, u32[]{:S(2)}) %collective-permute-start.7) | collective-permute-done | bytes 524320 | tf_op jit(solution)/shard_map/ppermute | solution.py:353
  230.9 10.2 %collective-permute-done.8.refs_1_ = bf16[2,128,1024]{2,1,0:T(8,128)(2,1)S(1)} collective-permute-done((bf16[2,128,1024]{2,1,0:T(8,128)(2,1)S(1)}, bf16[2,128,1024]{2,1,0:T(8,128)(2,1)S(1)}, u32[]{:S(2)}, u32[]{:S(2)}) %collective-permute-start.8) | collective-permute-done | bytes 524320 | tf_op jit(solution)/shard_map/ppermute | solution.py:353
  243.0 19.1 %layer.6 = (bf16[4,160,1024]{2,1,0:T(8,128)(2,1)}, bf16[4,160,1024]{2,1,0:T(8,128)(2,1)}) custom-call(s32[1,128]{1,0:T(1,128)} %add_bitcast_fusion.own_ref, s32[2,128]{1,0:T(2,128)} %get-tuple-element.22.table, bf16[3,32,1024]{2,1,0:T(8,128)(2,1)} %question_projections.1.question, bf16[2,1,1024]{2,1,0:T(2,128)(2,1)} %reshape.4.gain, ...), custom_call_target="tpu_custom_call" | custom-call | flops 9126805504 | bytes 16777216 | tf_op jit(solution)/shard_map/layer/pallas_call | solution.py:260
  263.8 20.4 %layer.5 = (bf16[4,160,1024]{2,1,0:T(8,128)(2,1)}, bf16[4,160,1024]{2,1,0:T(8,128)(2,1)}) custom-call(s32[1,128]{1,0:T(1,128)} %add_bitcast_fusion.own_ref, s32[2,128]{1,0:T(2,128)} %get-tuple-element.22.table, bf16[3,32,1024]{2,1,0:T(8,128)(2,1)} %question_projections.1.question, bf16[2,1,1024]{2,1,0:T(2,128)(2,1)} %reshape.4.gain, ...), custom_call_target="tpu_custom_call" | custom-call | flops 9126805504 | bytes 16777216 | tf_op jit(solution)/shard_map/layer/pallas_call | solution.py:260
  286.2 18.9 %layer.4 = (bf16[4,160,1024]{2,1,0:T(8,128)(2,1)}, bf16[4,160,1024]{2,1,0:T(8,128)(2,1)}) custom-call(s32[1,128]{1,0:T(1,128)} %add_bitcast_fusion.own_ref, s32[2,128]{1,0:T(2,128)} %get-tuple-element.22.table, bf16[3,32,1024]{2,1,0:T(8,128)(2,1)} %question_projections.1.question, bf16[2,1,1024]{2,1,0:T(2,128)(2,1)} %reshape.4.gain, ...), custom_call_target="tpu_custom_call" | custom-call | flops 9126805504 | bytes 16777216 | tf_op jit(solution)/shard_map/layer/pallas_call | solution.py:260
  305.4 1.1 copy-done.4
  306.4 3.1 combine.4.refs_4_
  309.6 1.1 copy-done.1
  310.7 3.3 %combine.5.refs_4_ = bf16[1,12,160,1024]{3,2,1,0:T(8,128)(2,1)} custom-call(s32[1,128]{1,0:T(1,128)} %add_bitcast_fusion.own_ref, s32[2,128]{1,0:T(2,128)} %get-tuple-element.22.table, bf16[1,32,1024]{2,1,0:T(8,128)(2,1)} %questions.7, bf16[2,128,1024]{2,1,0:T(8,128)(2,1)} %copy-done.6, ...), custom_call_target="tpu_custom_call", output_to_operand_aliasing={{}: (7, {})} | custom-call | bytes 5242880 | tf_op jit(solution)/shard_map/combine/pallas_call | solution.py:324
  314.0 1.1 copy-done.2
  315.1 3.4 %combine.6.refs_4_ = bf16[1,12,160,1024]{3,2,1,0:T(8,128)(2,1)} custom-call(s32[1,128]{1,0:T(1,128)} %add_bitcast_fusion.own_ref, s32[2,128]{1,0:T(2,128)} %get-tuple-element.22.table, bf16[1,32,1024]{2,1,0:T(8,128)(2,1)} %questions.7, bf16[2,128,1024]{2,1,0:T(8,128)(2,1)} %copy-done.7, ...), custom_call_target="tpu_custom_call", output_to_operand_aliasing={{}: (7, {})} | custom-call | bytes 5242880 | tf_op jit(solution)/shard_map/combine/pallas_call | solution.py:324
  318.5 1.1 copy-done.3
  319.6 3.3 %combine.7 = bf16[1,12,160,1024]{3,2,1,0:T(8,128)(2,1)} custom-call(s32[1,128]{1,0:T(1,128)} %add_bitcast_fusion.own_ref, s32[2,128]{1,0:T(2,128)} %get-tuple-element.22.table, bf16[1,32,1024]{2,1,0:T(8,128)(2,1)} %questions.7, bf16[2,128,1024]{2,1,0:T(8,128)(2,1)} %copy-done.9, bf16[2,128,1024]{2,1,0:T(8,128)(2,1)} %copy-done.11, ...), custom_call_target="tpu_custom_call", output_to_operand_aliasing={{}: (7, {})} | custom-call | bytes 5242880 | tf_op jit(solution)/shard_map/combine/pallas_call | solution.py:324
  (103 shorter events, 11.7 us)
Async XLA Ops:
  0.8 6.6 %collective-permute-start = (s32[1,128]{1,0:T(1,128)S(1)}, s32[1,128]{1,0:T(1,128)S(1)}, u32[]{:S(2)}, u32[]{:S(2)}) collective-permute-start(s32[1,128]{1,0:T(1,128)S(1)} %add_bitcast_fusion.1.refs_0_), channel_id=1, source_target_pairs={{0,2},{2,0},{4,6},{6,4},{8,10},{10,8},{12,14},{14,12},{1,3},{3,1},... | collective-permute-start | bytes 1544 | tf_op jit(solution)/shard_map/ppermute | solution.py:353
  2.0 6.8 %collective-permute-start.1 = (s32[1,128]{1,0:T(1,128)S(1)}, s32[1,128]{1,0:T(1,128)S(1)}, u32[]{:S(2)}, u32[]{:S(2)}) collective-permute-start(s32[1,128]{1,0:T(1,128)S(1)} %add_bitcast_fusion.1.refs_0_), channel_id=1, source_target_pairs={{0,4},{2,6},{4,0},{6,2},{8,12},{10,14},{12,8},{14,10},{1,5},{3,7},... | collective-permute-start | bytes 1544 | tf_op jit(solution)/shard_map/ppermute | solution.py:353
  2.2 7.3 %collective-permute-start.2 = (s32[1,128]{1,0:T(1,128)S(1)}, s32[1,128]{1,0:T(1,128)S(1)}, u32[]{:S(2)}, u32[]{:S(2)}) collective-permute-start(s32[1,128]{1,0:T(1,128)S(1)} %add_bitcast_fusion.1.refs_0_), channel_id=1, source_target_pairs={{0,6},{2,4},{4,2},{6,0},{8,14},{10,12},{12,10},{14,8},{1,7},{3,5},... | collective-permute-start | bytes 1544 | tf_op jit(solution)/shard_map/ppermute | solution.py:353
  3.4 6.1 %collective-permute-start.3 = (s32[1,128]{1,0:T(1,128)S(1)}, s32[1,128]{1,0:T(1,128)S(1)}, u32[]{:S(2)}, u32[]{:S(2)}) collective-permute-start(s32[1,128]{1,0:T(1,128)S(1)} %add_bitcast_fusion.1.refs_0_), channel_id=1, source_target_pairs={{0,8},{2,10},{4,12},{6,14},{8,0},{10,2},{12,4},{14,6},{1,9},{3,11}... | collective-permute-start | bytes 1544 | tf_op jit(solution)/shard_map/ppermute | solution.py:353
  5.7 4.2 %collective-permute-start.4 = (s32[1,128]{1,0:T(1,128)S(1)}, s32[1,128]{1,0:T(1,128)S(1)}, u32[]{:S(2)}, u32[]{:S(2)}) collective-permute-start(s32[1,128]{1,0:T(1,128)S(1)} %add_bitcast_fusion.1.refs_0_), channel_id=1, source_target_pairs={{0,10},{2,8},{4,14},{6,12},{8,2},{10,0},{12,6},{14,4},{1,11},{3,9}... | collective-permute-start | bytes 1544 | tf_op jit(solution)/shard_map/ppermute | solution.py:353
  7.4 2.5 collective-permute-start.5
  8.8 3.3 %collective-permute-start.6 = (s32[1,128]{1,0:T(1,128)S(1)}, s32[1,128]{1,0:T(1,128)S(1)}, u32[]{:S(2)}, u32[]{:S(2)}) collective-permute-start(s32[1,128]{1,0:T(1,128)S(1)} %add_bitcast_fusion.1.refs_0_), channel_id=1, source_target_pairs={{0,14},{2,12},{4,10},{6,8},{8,6},{10,4},{12,2},{14,0},{1,15},{3,13... | collective-permute-start | bytes 1544 | tf_op jit(solution)/shard_map/ppermute | solution.py:353
  9.5 117.0 %copy-start = (bf16[1,32,1024]{2,1,0:T(8,128)(2,1)S(1)}, bf16[1,32,1024]{2,1,0:T(8,128)(2,1)}, u32[]{:S(2)}) copy-start(bf16[1,32,1024]{2,1,0:T(8,128)(2,1)} %questions.7) | copy-start | bytes 196612
  9.5 133.9 %copy-start.13 = (bf16[2048]{0:T(1024)(128)(2,1)S(1)}, bf16[2048]{0:T(1024)(128)(2,1)}, u32[]{:S(2)}) copy-start(bf16[2048]{0:T(1024)(128)(2,1)} %param.15) | copy-start | bytes 12292
  126.4 16.1 %collective-permute-start.23 = (bf16[2,128,1024]{2,1,0:T(8,128)(2,1)}, bf16[2,128,1024]{2,1,0:T(8,128)(2,1)S(1)}, u32[]{:S(2)}, u32[]{:S(2)}) collective-permute-start(bf16[2,128,1024]{2,1,0:T(8,128)(2,1)} %get-tuple-element.36), channel_id=1, source_target_pairs={{0,2},{2,0},{4,6},{6,4},{8,10},{10,8},{12,14},{14,12},{1,3},{3,1},... | collective-permute-start | bytes 1572872 | tf_op jit(solution)/shard_map/ppermute | solution.py:353
  126.5 15.9 %collective-permute-start.9 = (bf16[1,32,1024]{2,1,0:T(8,128)(2,1)S(1)}, bf16[1,32,1024]{2,1,0:T(8,128)(2,1)S(1)}, u32[]{:S(2)}, u32[]{:S(2)}) collective-permute-start(bf16[1,32,1024]{2,1,0:T(8,128)(2,1)S(1)} %copy-done), channel_id=1, source_target_pairs={{0,1},{1,0},{2,3},{3,2},{4,5},{5,4},{6,7},{7,6},{8,9},{9,8},{10,11... | collective-permute-start | bytes 196616 | tf_op jit(solution)/shard_map/ppermute | solution.py:350
  130.1 21.1 %collective-permute-start.24 = (bf16[2,128,1024]{2,1,0:T(8,128)(2,1)}, bf16[2,128,1024]{2,1,0:T(8,128)(2,1)S(1)}, u32[]{:S(2)}, u32[]{:S(2)}) collective-permute-start(bf16[2,128,1024]{2,1,0:T(8,128)(2,1)} %get-tuple-element.35.refs_0_), channel_id=1, source_target_pairs={{0,1},{1,0},{2,3},{3,2},{4,5},{5,4},{6,7},{7,6},{8,9},{9,8},{10,11... | collective-permute-start | bytes 1572872 | tf_op jit(solution)/shard_map/ppermute | solution.py:350
  130.2 35.2 %collective-permute-start.18 = (bf16[2,128,1024]{2,1,0:T(8,128)(2,1)}, bf16[2,128,1024]{2,1,0:T(8,128)(2,1)S(1)}, u32[]{:S(2)}, u32[]{:S(2)}) collective-permute-start(bf16[2,128,1024]{2,1,0:T(8,128)(2,1)} %get-tuple-element.31), channel_id=1, source_target_pairs={{0,4},{2,6},{4,0},{6,2},{8,12},{10,14},{12,8},{14,10},{1,5},{3,7},... | collective-permute-start | bytes 1572872 | tf_op jit(solution)/shard_map/ppermute | solution.py:353
  142.4 34.1 %collective-permute-start.19 = (bf16[2,128,1024]{2,1,0:T(8,128)(2,1)}, bf16[2,128,1024]{2,1,0:T(8,128)(2,1)S(1)}, u32[]{:S(2)}, u32[]{:S(2)}) collective-permute-start(bf16[2,128,1024]{2,1,0:T(8,128)(2,1)} %get-tuple-element.32), channel_id=1, source_target_pairs={{0,6},{2,4},{4,2},{6,0},{8,14},{10,12},{12,10},{14,8},{1,7},{3,5},... | collective-permute-start | bytes 1572872 | tf_op jit(solution)/shard_map/ppermute | solution.py:353
  142.4 40.7 %collective-permute-start.13 = (bf16[2,128,1024]{2,1,0:T(8,128)(2,1)}, bf16[2,128,1024]{2,1,0:T(8,128)(2,1)S(1)}, u32[]{:S(2)}, u32[]{:S(2)}) collective-permute-start(bf16[2,128,1024]{2,1,0:T(8,128)(2,1)} %get-tuple-element.27), channel_id=1, source_target_pairs={{0,8},{2,10},{4,12},{6,14},{8,0},{10,2},{12,4},{14,6},{1,9},{3,11}... | collective-permute-start | bytes 1572872 | tf_op jit(solution)/shard_map/ppermute | solution.py:353
  142.5 41.9 %collective-permute-start.25 = (bf16[2,128,1024]{2,1,0:T(8,128)(2,1)S(1)}, bf16[2,128,1024]{2,1,0:T(8,128)(2,1)S(1)}, u32[]{:S(2)}, u32[]{:S(2)}) collective-permute-start(bf16[2,128,1024]{2,1,0:T(8,128)(2,1)S(1)} %collective-permute-done.23.refs_1_), channel_id=1, source_target_pairs={{0,1},{1,0},{2,3},{3,2},{4,5},{5,4},{6,7},{7,6},{8,9},{9,8},{10,11... | collective-permute-start | bytes 1572872 | tf_op jit(solution)/shard_map/ppermute | solution.py:350
  151.2 33.3 %copy-start.25 = (bf16[2,128,1024]{2,1,0:T(8,128)(2,1)}, bf16[2,128,1024]{2,1,0:T(8,128)(2,1)S(1)}, u32[]{:S(2)}) copy-start(bf16[2,128,1024]{2,1,0:T(8,128)(2,1)S(1)} %collective-permute-done.24.refs_2_) | copy-start | bytes 1572868
  151.3 59.6 %collective-permute-start.14 = (bf16[2,128,1024]{2,1,0:T(8,128)(2,1)S(1)}, bf16[2,128,1024]{2,1,0:T(8,128)(2,1)S(1)}, u32[]{:S(2)}, u32[]{:S(2)}) collective-permute-start(bf16[2,128,1024]{2,1,0:T(8,128)(2,1)S(1)} %copy-done.24), channel_id=1, source_target_pairs={{0,10},{2,8},{4,14},{6,12},{8,2},{10,0},{12,6},{14,4},{1,11},{3,9}... | collective-permute-start | bytes 1572872 | tf_op jit(solution)/shard_map/ppermute | solution.py:353
  165.3 37.8 %copy-start.6 = (bf16[2,128,1024]{2,1,0:T(8,128)(2,1)}, bf16[2,128,1024]{2,1,0:T(8,128)(2,1)S(1)}, u32[]{:S(2)}) copy-start(bf16[2,128,1024]{2,1,0:T(8,128)(2,1)S(1)} %collective-permute-done.18.refs_0_) | copy-start | bytes 1572868
  165.3 64.7 %collective-permute-start.7 = (bf16[2,128,1024]{2,1,0:T(8,128)(2,1)S(1)}, bf16[2,128,1024]{2,1,0:T(8,128)(2,1)S(1)}, u32[]{:S(2)}, u32[]{:S(2)}) collective-permute-start(bf16[2,128,1024]{2,1,0:T(8,128)(2,1)S(1)} %copy-done.23), channel_id=1, source_target_pairs={{0,12},{2,14},{4,8},{6,10},{8,4},{10,6},{12,0},{14,2},{1,13},{3,15... | collective-permute-start | bytes 1572872 | tf_op jit(solution)/shard_map/ppermute | solution.py:353
  176.6 64.6 %collective-permute-start.8 = (bf16[2,128,1024]{2,1,0:T(8,128)(2,1)S(1)}, bf16[2,128,1024]{2,1,0:T(8,128)(2,1)S(1)}, u32[]{:S(2)}, u32[]{:S(2)}) collective-permute-start(bf16[2,128,1024]{2,1,0:T(8,128)(2,1)S(1)} %copy-done.22), channel_id=1, source_target_pairs={{0,14},{2,12},{4,10},{6,8},{8,6},{10,4},{12,2},{14,0},{1,15},{3,13... | collective-permute-start | bytes 1572872 | tf_op jit(solution)/shard_map/ppermute | solution.py:353
  183.1 58.9 %collective-permute-start.20 = (bf16[2,128,1024]{2,1,0:T(8,128)(2,1)S(1)}, bf16[2,128,1024]{2,1,0:T(8,128)(2,1)S(1)}, u32[]{:S(2)}, u32[]{:S(2)}) collective-permute-start(bf16[2,128,1024]{2,1,0:T(8,128)(2,1)S(1)} %collective-permute-done.18.refs_0_), channel_id=1, source_target_pairs={{0,1},{1,0},{2,3},{3,2},{4,5},{5,4},{6,7},{7,6},{8,9},{9,8},{10,11... | collective-permute-start | bytes 1572872 | tf_op jit(solution)/shard_map/ppermute | solution.py:350
  184.5 57.7 %collective-permute-start.21 = (bf16[2,128,1024]{2,1,0:T(8,128)(2,1)S(1)}, bf16[2,128,1024]{2,1,0:T(8,128)(2,1)S(1)}, u32[]{:S(2)}, u32[]{:S(2)}) collective-permute-start(bf16[2,128,1024]{2,1,0:T(8,128)(2,1)S(1)} %collective-permute-done.19.refs_1_), channel_id=1, source_target_pairs={{0,1},{1,0},{2,3},{3,2},{4,5},{5,4},{6,7},{7,6},{8,9},{9,8},{10,11... | collective-permute-start | bytes 1572872 | tf_op jit(solution)/shard_map/ppermute | solution.py:350
  210.8 51.3 %copy-start.10 = (bf16[2,128,1024]{2,1,0:T(8,128)(2,1)}, bf16[2,128,1024]{2,1,0:T(8,128)(2,1)S(1)}, u32[]{:S(2)}) copy-start(bf16[2,128,1024]{2,1,0:T(8,128)(2,1)S(1)} %collective-permute-done.14.refs_1_) | copy-start | bytes 1572868
  210.8 51.3 %collective-permute-start.15 = (bf16[2,128,1024]{2,1,0:T(8,128)(2,1)S(1)}, bf16[2,128,1024]{2,1,0:T(8,128)(2,1)S(1)}, u32[]{:S(2)}, u32[]{:S(2)}) collective-permute-start(bf16[2,128,1024]{2,1,0:T(8,128)(2,1)S(1)} %collective-permute-done.13.refs_0_), channel_id=1, source_target_pairs={{0,1},{1,0},{2,3},{3,2},{4,5},{5,4},{6,7},{7,6},{8,9},{9,8},{10,11... | collective-permute-start | bytes 1572872 | tf_op jit(solution)/shard_map/ppermute | solution.py:350
  230.0 32.6 %collective-permute-start.16 = (bf16[2,128,1024]{2,1,0:T(8,128)(2,1)S(1)}, bf16[2,128,1024]{2,1,0:T(8,128)(2,1)S(1)}, u32[]{:S(2)}, u32[]{:S(2)}) collective-permute-start(bf16[2,128,1024]{2,1,0:T(8,128)(2,1)S(1)} %collective-permute-done.14.refs_1_), channel_id=1, source_target_pairs={{0,1},{1,0},{2,3},{3,2},{4,5},{5,4},{6,7},{7,6},{8,9},{9,8},{10,11... | collective-permute-start | bytes 1572872 | tf_op jit(solution)/shard_map/ppermute | solution.py:350
  241.2 43.4 %collective-permute-start.10 = (bf16[2,128,1024]{2,1,0:T(8,128)(2,1)S(1)}, bf16[2,128,1024]{2,1,0:T(8,128)(2,1)S(1)}, u32[]{:S(2)}, u32[]{:S(2)}) collective-permute-start(bf16[2,128,1024]{2,1,0:T(8,128)(2,1)S(1)} %collective-permute-done.7.refs_0_), channel_id=1, source_target_pairs={{0,1},{1,0},{2,3},{3,2},{4,5},{5,4},{6,7},{7,6},{8,9},{9,8},{10,11... | collective-permute-start | bytes 1572872 | tf_op jit(solution)/shard_map/ppermute | solution.py:350
  242.0 42.6 %collective-permute-start.11 = (bf16[2,128,1024]{2,1,0:T(8,128)(2,1)S(1)}, bf16[2,128,1024]{2,1,0:T(8,128)(2,1)S(1)}, u32[]{:S(2)}, u32[]{:S(2)}) collective-permute-start(bf16[2,128,1024]{2,1,0:T(8,128)(2,1)S(1)} %collective-permute-done.8.refs_1_), channel_id=1, source_target_pairs={{0,1},{1,0},{2,3},{3,2},{4,5},{5,4},{6,7},{7,6},{8,9},{9,8},{10,11... | collective-permute-start | bytes 1572872 | tf_op jit(solution)/shard_map/ppermute | solution.py:350
  242.1 63.3 %collective-permute-start.26 = (bf16[4,160,1024]{2,1,0:T(8,128)(2,1)}, bf16[4,160,1024]{2,1,0:T(8,128)(2,1)S(1)}, u32[]{:S(2)}, u32[]{:S(2)}) collective-permute-start(bf16[4,160,1024]{2,1,0:T(8,128)(2,1)} %get-tuple-element.38), channel_id=1, source_target_pairs={{0,1},{1,0},{2,3},{3,2},{4,5},{5,4},{6,7},{7,6},{8,9},{9,8},{10,11... | collective-permute-start | bytes 3932168 | tf_op jit(solution)/shard_map/ppermute | solution.py:350
  262.2 47.4 %collective-permute-start.22 = (bf16[4,160,1024]{2,1,0:T(8,128)(2,1)}, bf16[4,160,1024]{2,1,0:T(8,128)(2,1)S(1)}, u32[]{:S(2)}, u32[]{:S(2)}) collective-permute-start(bf16[4,160,1024]{2,1,0:T(8,128)(2,1)} %get-tuple-element.34), channel_id=1, source_target_pairs={{0,1},{1,0},{2,3},{3,2},{4,5},{5,4},{6,7},{7,6},{8,9},{9,8},{10,11... | collective-permute-start | bytes 3932168 | tf_op jit(solution)/shard_map/ppermute | solution.py:350
  284.2 29.8 %collective-permute-start.17 = (bf16[4,160,1024]{2,1,0:T(8,128)(2,1)}, bf16[4,160,1024]{2,1,0:T(8,128)(2,1)S(1)}, u32[]{:S(2)}, u32[]{:S(2)}) collective-permute-start(bf16[4,160,1024]{2,1,0:T(8,128)(2,1)} %get-tuple-element.30), channel_id=1, source_target_pairs={{0,1},{1,0},{2,3},{3,2},{4,5},{5,4},{6,7},{7,6},{8,9},{9,8},{10,11... | collective-permute-start | bytes 3932168 | tf_op jit(solution)/shard_map/ppermute | solution.py:350
  305.1 13.4 %collective-permute-start.12 = (bf16[4,160,1024]{2,1,0:T(8,128)(2,1)}, bf16[4,160,1024]{2,1,0:T(8,128)(2,1)S(1)}, u32[]{:S(2)}, u32[]{:S(2)}) collective-permute-start(bf16[4,160,1024]{2,1,0:T(8,128)(2,1)} %get-tuple-element.26), channel_id=1, source_target_pairs={{0,1},{1,0},{2,3},{3,2},{4,5},{5,4},{6,7},{7,6},{8,9},{9,8},{10,11... | collective-permute-start | bytes 3932168 | tf_op jit(solution)/shard_map/ppermute | solution.py:350
  (28 other events, 218.3 us)
